TPU v7x, 256 devices: a whole 4x4x8 slice. The times are simulated.
256 devices in a mesh: region: 32 (over x, y, core), vel: 8 (over z).
Axes of the slice: x: 4, y: 4, z: 8, core: 2. Of those that a mesh axis runs over, the one named last changes fastest.
Arguments:
- distribution: float32 [32, 8192, 384], P('region', 'vel'), may hold values from 0.05 to 2
- velocity: float32 [32, 3, 8192], P('region', None, 'vel'), may hold values from 0.3 to 6
- weights: float32 [32, 8192], P('region', 'vel'), may hold values from 0.012207031 to 0.048828125
- grid_points: int32 [32], replicated, may hold values from 1024 to 8192, as said below
- neighbours: int32 [32, 5], replicated, may hold values from 0 to 31, as said below
- interface_cells: int32 [32, 5, 16], P('region'), may hold values from 0 to 383
- interpolation: float32 [32, 5, 8192, 128], P('region', None, 'vel'), may hold values from 0 to 1
- block_inverse: float32 [32, 64, 384, 384], P('region', 'vel'), may hold values from 0 to 1
Outputs:
- updated: float32 [32, 8192, 384], P('region', 'vel')
Inputs may be any that keep to these rules, and one draw needn't show every extreme that they name: `grid_points`: multiples of 128; one region has exactly 8192 points and another exactly the least. Row r lists r + 1, r - 1, r + B, r - B and r + 16, all modulo 32, for one offset B of 2 to 15 drawn anew in each draw; so every region is listed by each of its neighbours.
All inputs are finite; a program needn't handle non-finite values.
Results may differ from a plain program's by a relative error of at most 0.0003.
Values sent between devices are 32-bit elements; how exact they have to be, the bound alone decides.
A program may use at most 64 MiB of HBM per device.

v0:
```python
import functools
import math

import jax
import jax.numpy as jnp
from jax import lax
from jax.experimental import pallas as pl
from jax.experimental.pallas import tpu as pltpu
from jax.sharding import PartitionSpec as P

VMAX = 8192
BLK = 128
EDGE = 16
NBR = 5
ITERS = 2
PAD = 128
WIDE = 256
BASIS = 16
TILE = 8

relax_step = 0.5
inflow_step = 0.5
viscous_conductive_ratio = 2.0 / 3.0

MESH = pl.DeviceIdType.MESH
f32 = jnp.float32
bf16 = jnp.bfloat16


def across(a, b):
    return lax.dot_general(a, b, (((1,), (1,)), ((), ())), preferred_element_type=f32)


def plain(a, b):
    return jnp.dot(a, b, preferred_element_type=f32)


def halves(x):
    high = x.astype(bf16)
    return high, (x - high.astype(f32)).astype(bf16)


def moment_rows(x, y, z):
    speed_sq = x * x + y * y + z * z
    return [
        jnp.ones_like(x), x, y, z,
        x * x, y * y, z * z,
        x * y, x * z, y * z,
        x * speed_sq, y * speed_sq, z * speed_sq,
    ]


def cell_rows(m):
    density = m[0]
    over = 1.0 / density
    u, v, w = m[1] * over, m[2] * over, m[3] * over
    energy = m[4] + m[5] + m[6]
    flow_sq = u * u + v * v + w * w
    warmth = (energy * over - flow_sq) / 3.0
    stress_x = m[4] * u + m[7] * v + m[8] * w
    stress_y = m[7] * u + m[5] * v + m[9] * w
    stress_z = m[8] * u + m[9] * v + m[6] * w
    drift = 2.0 * density * flow_sq
    heat_x = 0.5 * (m[10] - 2.0 * stress_x - u * energy + drift * u)
    heat_y = 0.5 * (m[11] - 2.0 * stress_y - v * energy + drift * v)
    heat_z = 0.5 * (m[12] - 2.0 * stress_z - w * energy + drift * w)
    hot = 2.0 * math.pi * warmth
    front = relax_step * density / (hot * jnp.sqrt(hot))
    fall = -0.5 / warmth
    skew = (-2.0 * (1.0 - viscous_conductive_ratio)) / (5.0 * density * warmth * warmth)
    return [front, u, v, w, fall, heat_x * skew, heat_y * skew, heat_z * skew]


def kernel(
    regions, shards, unroll,
    dist_hbm, vel_hbm, weights_hbm, points, neighbours, cells, interp_hbm, inv_hbm, out_hbm,
    dist, vel, weights, interp, inv, both_inv, both_edge, edge_edge, inv_edge, mats,
    basis_f, basis, columns, onehot_f, onehot, halved, pieces, flow_t, flow, kept, sent, recv, tiles, hold_a, hold_b, moved, reached, part, gathered, coef, rhs, result,
    in_sem, out_sem, edge_send, edge_recv, hop_send, hop_recv, part_send, part_recv,
):
    region = lax.axis_index("region")
    shard = lax.axis_index("vel")
    local, cell_count = dist.shape
    blocks = local // BLK
    width = NBR * EDGE

    loads = [
        pltpu.make_async_copy(source, target, in_sem.at[i])
        for i, (source, target) in enumerate(
            [
                (dist_hbm.at[0], dist),
                (vel_hbm, vel),
                (weights_hbm, weights),
                (inv_hbm.at[0], inv),
                (interp_hbm.at[0], interp),
            ]
        )
    ]
    for load in loads:
        load.start()

    def shifted(offset):
        return lax.rem(region + offset + regions, regions)

    peers = [lax.rem(shard + step, shards) for step in range(1, shards)]
    barrier = pltpu.get_barrier_semaphore()

    def others(body):
        def one(offset, carry):
            body(shifted(offset))
            return carry

        lax.fori_loop(1, regions, one, 0)

    others(lambda r: pl.semaphore_signal(barrier, inc=1, device_id=(r, shard), device_id_type=MESH))
    for peer in peers:
        pl.semaphore_signal(barrier, inc=1, device_id=(region, peer), device_id_type=MESH)

    def remote(source, target, send, arrive, device):
        return pltpu.make_async_remote_copy(
            src_ref=source, dst_ref=target, send_sem=send, recv_sem=arrive, device_id=device, device_id_type=MESH
        )

    def slot_rows(k):
        return pl.ds(EDGE * k, EDGE)

    direct_copies = [
        [
            remote(
                sent.at[turn, slot_rows(k)], recv.at[turn, j], edge_send.at[turn, j], edge_recv.at[turn, j],
                (shifted(offset), shard),
            )
            for j, (k, offset) in enumerate(((1, -1), (0, 1), (4, regions // 2)))
        ]
        for turn in range(ITERS)
    ]
    hold = (hold_a, hold_b)

    def out_copy(turn, r):
        return remote(tiles.at[turn, r], hold[turn].at[region], hop_send.at[turn, 0], hop_recv.at[turn, 0], (r, shard))

    def on_copy(turn, r):
        return remote(moved.at[turn, r], reached.at[turn, region], hop_send.at[turn, 1], hop_recv.at[turn, 1], (r, shard))

    def all_tiles(turn, step):
        ref = (hold[turn] if step == 0 else reached.at[turn]).at[pl.ds(0, regions - 1)]
        return remote(ref, ref, hop_send.at[turn, step], hop_recv.at[turn, step], (shifted(1), shard))

    part_copies = [
        [
            remote(part.at[turn], gathered.at[turn, j], part_send.at[turn, j], part_recv.at[turn, j], (region, peers[j]))
            for j in range(shards - 1)
        ]
        for turn in range(ITERS)
    ]

    total = points[region]
    stride = lax.rem(neighbours[2, 0] + regions, regions)
    backward = jnp.where(region < regions // 2, regions - stride, stride)

    def alive(n):
        return jnp.where((shard * blocks + n) * BLK < total, f32(1.0), f32(0.0))

    def rows_of(n):
        return pl.ds(pl.multiple_of(n * BLK, BLK), BLK)

    def each(body, init=0):
        return lax.fori_loop(0, blocks, body, init, unroll=unroll)

    def post_edges(turn, n, edges):
        sent[turn, :, rows_of(n)] = edges
        for group in range(regions // blocks):
            start = 2 * EDGE + TILE * group
            tiles[turn, group * blocks + n] = edges[start : start + TILE]

    def send_edges(turn):
        hold[turn][region] = tiles[turn, region]
        others(lambda r: out_copy(turn, r).start())
        for copy in direct_copies[turn]:
            copy.start()

    def send_part(turn, total_part):
        part[turn] = total_part
        for copy in part_copies[turn]:
            copy.start()

    with jax.named_scope("onehot"):
        onehot_f[...] = jnp.zeros_like(onehot_f)
        lane = lax.broadcasted_iota(jnp.int32, (1, cell_count), 1)
        for k in range(NBR):
            for i in range(EDGE):
                row = EDGE * k + i
                onehot_f[row : row + 1, :] = (lane == cells[k, 0, i]).astype(f32)
        picks = onehot_f[...]
        onehot[...] = picks.astype(bf16)
        half = (inflow_step * picks[0:width]).astype(bf16)
        halved[3 * width :, :] = jnp.zeros((WIDE - 3 * width, cell_count), bf16)
        for i in range(3):
            halved[i * width : (i + 1) * width, :] = half

    with jax.named_scope("wait_dist"):
        loads[0].wait()

    def first_edges(n, carry):
        high, low = halves(dist[rows_of(n), :] * alive(n))
        pick = onehot[0:width]
        post_edges(0, n, across(pick, high) + across(pick, low))
        return carry

    with jax.named_scope("first_edges"):
        each(first_edges)

    with jax.named_scope("entry"):
        pl.semaphore_wait(barrier, regions + shards - 2)
        send_edges(0)

    with jax.named_scope("basis"):
        loads[1].wait()
        loads[2].wait()
        x, y, z = vel[0], vel[1], vel[2]
        place = shard * local + lax.broadcasted_iota(jnp.int32, (1, local), 1)
        scale = f32(VMAX) / jnp.full((1, local), total.astype(f32))
        quad = weights[...] * scale * (place < total).astype(f32)
        basis_f[...] = jnp.zeros_like(basis_f)
        for i, row in enumerate(moment_rows(x, y, z)):
            basis_f[i : i + 1, :] = row * quad

        def split_basis(n, carry):
            high, low = halves(basis_f[:, rows_of(n)])
            basis[n, 0:BASIS, 0:BLK] = high
            basis[n, 0:BASIS, BLK : 2 * BLK] = high
            basis[n, BASIS : 2 * BASIS, 0:BLK] = low
            basis[n, BASIS : 2 * BASIS, BLK : 2 * BLK] = jnp.zeros_like(low)
            return carry

        each(split_basis)

    def weighted(n, high, low):
        both = plain(basis[n], jnp.concatenate([high, low], axis=0))
        return both[:BASIS] + both[BASIS:]

    def first_moments(n, acc):
        high, low = halves(dist[rows_of(n), :] * alive(n))
        return acc + weighted(n, high, low)

    with jax.named_scope("first_moments"):
        send_part(0, each(first_moments, jnp.zeros((BASIS, cell_count), f32)))

    with jax.named_scope("turn_columns"):
        basis_f[0:3, :] = jnp.concatenate([x, y, z], axis=0)

        def turn_columns(n, carry):
            turned = jnp.transpose(basis_f[0:8, rows_of(n)])
            for axis in range(3):
                columns[axis, rows_of(n), :] = jnp.broadcast_to(turned[:, axis : axis + 1], (BLK, 128))
            return carry

        each(turn_columns)
        pieces[...] = jnp.zeros_like(pieces)
        flow_t[...] = jnp.zeros_like(flow_t)

    def forward(turn):
        all_tiles(turn, 0).wait_recv()

        def take(r, carry):
            moved[turn, r] = hold[turn][lax.rem(r + backward, regions)]
            return carry

        lax.fori_loop(0, regions, take, 0, unroll=8)
        reached[turn, region] = moved[turn, region]
        others(lambda r: on_copy(turn, r).start())

    def prepare_inv(n, carry):
        high, low = halves(inv[n])
        both_inv[n, :, 0:cell_count] = high
        both_inv[n, :, cell_count : 2 * cell_count] = low
        edges = plain(onehot[0:width], jnp.concatenate([high, low], axis=1)).astype(bf16)
        both_edge[n, 0:width, 0:cell_count] = edges[:, 0:cell_count]
        both_edge[n, 0:width, cell_count : 2 * cell_count] = edges[:, 0:cell_count]
        both_edge[n, width : 2 * width, 0:cell_count] = edges[:, cell_count : 2 * cell_count]
        both_edge[n, width : 2 * width, cell_count : 2 * cell_count] = jnp.zeros((width, cell_count), bf16)
        back_h = across(halved[0:width], high).astype(bf16)
        inv_edge[n, 0:width] = back_h
        inv_edge[n, width : 2 * width] = back_h
        inv_edge[n, 2 * width : WIDE] = across(halved[2 * width : WIDE], low).astype(bf16)
        near = across(edges[:, 0:cell_count], halved[...])
        fine = across(edges[:, cell_count : 2 * cell_count], halved[...])
        lane = lax.broadcasted_iota(jnp.int32, (width, WIDE), 1)
        edge_edge[n] = jnp.where(lane < 2 * width, near, fine).astype(bf16)
        return carry

    def prepare_mat(n, carry):
        for k in range(NBR):
            high, low = halves(interp[k, rows_of(n), :])
            mats[n, k, :, 0:BLK] = high
            mats[n, k, :, BLK : 2 * BLK] = low
        return carry

    with jax.named_scope("prepare_inv"):
        loads[3].wait()
        each(prepare_inv)
    with jax.named_scope("forward0"):
        forward(0)
    with jax.named_scope("prepare_mat"):
        loads[4].wait()
        each(prepare_mat)

    def collect(turn):
        for copy in part_copies[turn]:
            copy.wait_recv()
        moments = part[turn]
        for j in range(shards - 1):
            moments = moments + gathered[turn, j]
        rows = cell_rows([moments[i : i + 1, :] for i in range(13)])
        for i, row in enumerate(rows):
            coef[i : i + 1, :] = row

    def relax(n, carry):
        on = alive(n)
        chunk = 32
        for tile in range(cell_count // 128):
            lanes = pl.ds(128 * tile, 128)
            front, u, v, w, fall, skew_x, skew_y, skew_z = [coef[i : i + 1, lanes] for i in range(8)]
            for c in range(BLK // chunk):
                rows = pl.ds(pl.multiple_of(n * BLK + c * chunk, chunk), chunk)
                e_x = columns[0, rows, :] - u
                e_y = columns[1, rows, :] - v
                e_z = columns[2, rows, :] - w
                power = (e_x * e_x + e_y * e_y + e_z * e_z) * fall
                lean = e_x * skew_x + e_y * skew_y + e_z * skew_z
                value = front * jnp.exp(power) * (1.0 + lean * (power + 2.5))
                rhs[rows, lanes] = dist[rows, lanes] * on + value
        return carry

    def place_in(k, value):
        high, low = halves(value)
        for n in range(blocks):
            lanes = slice(BLK * n, BLK * (n + 1))
            pieces[n, k, 0:EDGE, 0:BLK] = high[:, lanes]
            pieces[n, k, 0:EDGE, BLK : 2 * BLK] = high[:, lanes]
            pieces[n, k, EDGE : 2 * EDGE, 0:BLK] = low[:, lanes]

    def arrive(turn):
        for j, k in enumerate((0, 1, 4)):
            direct_copies[turn][j].wait_recv()
            place_in(k, recv[turn, j])
        all_tiles(turn, 1).wait_recv()
        for k, first in ((3, 0), (2, 2 * blocks)):
            rows = [[reached[turn, first + g * blocks + n] for n in range(blocks)] for g in range(2)]
            place_in(k, jnp.concatenate([jnp.concatenate(r, axis=1) for r in rows], axis=0))

    def interpolate(n, carry):
        flows = []
        for k in range(NBR):
            both = across(pieces[n, k], mats[n, k])
            flows.append(both[:EDGE] + both[EDGE:])
        high, low = halves(jnp.concatenate(flows, axis=0))
        flow_t[n, 0:width] = high
        flow_t[n, width : 2 * width] = low
        flow_t[n, 2 * width : 3 * width] = high
        flow[n] = jnp.transpose(flow_t[n])
        return carry

    with jax.named_scope("collect0"):
        collect(0)
    with jax.named_scope("relax0"):
        each(relax)

    def main_edges(n, carry):
        high, low = halves(rhs[rows_of(n), :])
        edges = across(both_edge[n], jnp.concatenate([high, low], axis=1))
        kept[n] = edges[:width] + edges[width:]
        return carry

    def main_moments(n, acc):
        high, low = halves(rhs[rows_of(n), :])
        held_h, held_l = halves(weighted(n, high, low))
        held = jnp.concatenate(
            [
                jnp.concatenate([held_h, held_h], axis=1),
                jnp.concatenate([held_l, jnp.zeros_like(held_l)], axis=1),
            ],
            axis=0,
        )
        both = across(held, both_inv[n])
        return acc + both[:BASIS] + both[BASIS:]

    with jax.named_scope("main_edges"):
        each(main_edges)
    with jax.named_scope("main_moments"):
        main_part = each(main_moments, jnp.zeros((BASIS, cell_count), f32))
    with jax.named_scope("arrive0"):
        arrive(0)
    with jax.named_scope("interpolate0"):
        each(interpolate)

    def landed_edges(n, carry):
        post_edges(1, n, (kept[n] + plain(edge_edge[n], flow_t[n])) * alive(n))
        return carry

    def landed_moments(n, acc):
        both = plain(basis[n, :, 0:BLK], flow[n])
        held_h, held_l = halves(both[:BASIS] + both[BASIS:])
        both = plain(jnp.concatenate([held_h, held_l], axis=0), inv_edge[n])
        return acc + both[:BASIS] + both[BASIS:]

    with jax.named_scope("landed_edges"):
        each(landed_edges)
        send_edges(1)
    with jax.named_scope("landed_moments"):
        send_part(1, each(landed_moments, main_part))
    with jax.named_scope("forward1"):
        forward(1)
    with jax.named_scope("collect1"):
        collect(1)
    with jax.named_scope("relax1"):
        each(relax)

    def main_result(n, carry):
        high, low = halves(rhs[rows_of(n), :])
        value = across(jnp.concatenate([high, high], axis=1), both_inv[n])
        result[rows_of(n), :] = value + across(low, both_inv[n, :, 0:cell_count])
        return carry

    def last(n, carry):
        result[rows_of(n), :] = (result[rows_of(n), :] + plain(flow[n], inv_edge[n])) * alive(n)
        pltpu.make_async_copy(result.at[rows_of(n)], out_hbm.at[0, rows_of(n)], out_sem.at[n]).start()
        return carry

    with jax.named_scope("main_result"):
        each(main_result)
    with jax.named_scope("arrive1"):
        arrive(1)
    with jax.named_scope("interpolate1"):
        each(interpolate)
    with jax.named_scope("last"):
        each(last)
    with jax.named_scope("finish"):
        for n in range(blocks):
            rows = pl.ds(n * BLK, BLK)
            pltpu.make_async_copy(result.at[rows], out_hbm.at[0, rows], out_sem.at[n]).wait()
        for turn in range(ITERS):
            for copy in part_copies[turn] + direct_copies[turn]:
                copy.wait_send()
            for step in range(2):
                all_tiles(turn, step).wait_send()


def update(regions, shards, unroll, *arrays):
    distribution, velocity, weights, points, neighbours, cells, interpolation, inverse = arrays
    local, cell_count = distribution.shape[1:]
    blocks = local // BLK
    width = NBR * EDGE
    anywhere = pl.BlockSpec(memory_space=pl.ANY)
    scalars = pl.BlockSpec(memory_space=pltpu.SMEM)
    vmem = pltpu.VMEM
    signals = pltpu.SemaphoreType.DMA
    return pl.pallas_call(
        functools.partial(kernel, regions, shards, unroll),
        out_shape=jax.ShapeDtypeStruct((1, local, cell_count), f32),
        in_specs=[anywhere, anywhere, anywhere, scalars, scalars, scalars, anywhere, anywhere],
        out_specs=anywhere,
        scratch_shapes=[
            vmem((local, cell_count), f32),
            vmem((3, 1, local), f32),
            vmem((1, local), f32),
            vmem((NBR, local, BLK), f32),
            vmem((blocks, cell_count, cell_count), f32),
            vmem((blocks, cell_count, 2 * cell_count), bf16),
            vmem((blocks, 2 * width, 2 * cell_count), bf16),
            vmem((blocks, width, WIDE), bf16),
            vmem((blocks, WIDE, cell_count), bf16),
            vmem((blocks, NBR, BLK, 2 * BLK), bf16),
            vmem((BASIS, local), f32),
            vmem((blocks, 2 * BASIS, 2 * BLK), bf16),
            vmem((3, local, 128), f32),
            vmem((PAD, cell_count), f32),
            vmem((PAD, cell_count), bf16),
            vmem((WIDE, cell_count), bf16),
            vmem((blocks, NBR, 2 * EDGE, 2 * BLK), bf16),
            vmem((blocks, WIDE, BLK), bf16),
            vmem((blocks, BLK, WIDE), bf16),
            vmem((blocks, width, BLK), f32),
            vmem((ITERS, width, local), f32),
            vmem((ITERS, 3, EDGE, local), f32),
            vmem((ITERS, regions, TILE, BLK), f32),
            vmem((regions, TILE, BLK), f32),
            vmem((regions, TILE, BLK), f32),
            vmem((ITERS, regions, TILE, BLK), f32),
            vmem((ITERS, regions, TILE, BLK), f32),
            vmem((ITERS, BASIS, cell_count), f32),
            vmem((ITERS, shards - 1, BASIS, cell_count), f32),
            vmem((8, cell_count), f32),
            vmem((local, cell_count), f32),
            vmem((local, cell_count), f32),
            signals((5,)),
            signals((blocks,)),
            signals((ITERS, 3)),
            signals((ITERS, 3)),
            signals((ITERS, 2)),
            signals((ITERS, 2)),
            signals((ITERS, shards - 1)),
            signals((ITERS, shards - 1)),
        ],
        compiler_params=pltpu.CompilerParams(
            collective_id=0, has_side_effects=True, vmem_limit_bytes=56 * 1024 * 1024
        ),
    )(distribution, velocity, weights, points, neighbours, cells, interpolation, inverse)


def solution(mesh):
    regions, shards = mesh.shape["region"], mesh.shape["vel"]

    def local(distribution, velocity, weights, grid_points, neighbours, interface_cells, interpolation, block_inverse):
        return update(
            regions, shards, 8,
            distribution, velocity.transpose(1, 0, 2), weights, grid_points, neighbours.T,
            interface_cells.transpose(1, 0, 2), interpolation, block_inverse,
        )

    placed = (
        P("region", "vel", None),
        P("region", None, "vel"),
        P("region", "vel"),
        P(),
        P(),
        P("region", None, None),
        P("region", None, "vel", None),
        P("region", "vel", None, None),
    )
    return jax.shard_map(
        local, mesh=mesh, in_specs=placed, out_specs=P("region", "vel", None), check_vma=False
    )
```

profile of v0, /device:TPU:1, one launch (start us, length us, event | category | flops | bytes accessed | tf_op | source)
XLA Modules:
  0.0 42.2 jit_solution(6972017839799875728)
XLA Ops:
  0.0 39.5 %shard_map.82 = f32[1,1024,384]{2,1,0:T(8,128)} custom-call(f32[1,1024,384]{2,1,0:T(8,128)} %dist_hbm.1, f32[3,1,1024]{2,1,0:T(1,128)} %bitcast.3, f32[1,1024]{1,0:T(1,128)} %weights_hbm.1, s32[32]{0:T(128)} %points.1, s32[5,32]{1,0:T(8,128)} %bitcast.4, s32[5,1,16]{2,1,0:T(1,128)} %bitcast.5, f32[1,5,1024,128]{3,2,1,0:T(8,128)} %interp_hbm.1, ...), custom_call_target="tpu_custom_call" | custom-call | tf_op jit(solution)/shard_map/pallas_call | solution.py:458
  39.5 2.7 %copy.10 = f32[1,1024,384]{2,1,0:T(8,128)} copy(f32[1,1024,384]{2,1,0:T(8,128)} %shard_map.82) | data formatting | bytes 3145728
where the time goes:
time: 42.3 us; the launch traced here: 42.2 us
  Pallas kernels  39.5 us (93%)
  local copies, waits for them, and re-layouts  2.65 us (6%)
    pallas_call x1, Pallas kernels, update(): pl.pallas_call(functools.partial(kernel, regions, shards, unroll), out_sh...  39.5 us
    unnamed x1, local copies, waits for them, and re-layouts  2.65 us

commit v1 on v0

--- a/solution.py
+++ b/solution.py
@@ -16,6 +16,7 @@
 PAD = 128
 WIDE = 256
 BASIS = 16
+MOMENTS = 13
 TILE = 8
 
 relax_step = 0.5
@@ -25,6 +26,20 @@
 MESH = pl.DeviceIdType.MESH
 f32 = jnp.float32
 bf16 = jnp.bfloat16
+
+
+def far_first(regions):
+    side = math.isqrt(regions // 2)
+
+    def hops(offset):
+        total = 0
+        for region in range(regions):
+            here, there = region // 2, (region + offset) % regions // 2
+            for a, b in ((here // side, there // side), (here % side, there % side)):
+                total += min((a - b) % side, (b - a) % side)
+        return total
+
+    return sorted(range(1, regions), key=lambda offset: (-hops(offset), offset))
 
 
 def across(a, b):
@@ -73,16 +88,32 @@
 
 def kernel(
     regions, shards, unroll,
-    dist_hbm, vel_hbm, weights_hbm, points, neighbours, cells, interp_hbm, inv_hbm, out_hbm,
-    dist, vel, weights, interp, inv, both_inv, both_edge, edge_edge, inv_edge, mats,
-    basis_f, basis, columns, onehot_f, onehot, halved, pieces, flow_t, flow, kept, sent, recv, tiles, hold_a, hold_b, moved, reached, part, gathered, coef, rhs, result,
-    in_sem, out_sem, edge_send, edge_recv, hop_send, hop_recv, part_send, part_recv,
+    dist_hbm, vel_hbm, weights_hbm, points_hbm, neighbours_hbm, cells_hbm, interp_hbm, inv_hbm, out,
+    points, neighbours, cells, dist, vel, weights, interp, inv, both_inv, both_edge, edge_edge, inv_edge, mats,
+    basis_f, basis, columns, onehot_f, onehot, halved, pieces, flow_t, flow, kept, sent, recv, tiles, hold_a, hold_b, moved, reached, part, gathered, coef, rhs,
+    in_sem, edge_send, edge_recv, hop_send, hop_recv, part_send, part_recv,
 ):
     region = lax.axis_index("region")
     shard = lax.axis_index("vel")
     local, cell_count = dist.shape
     blocks = local // BLK
     width = NBR * EDGE
+
+    def shifted(offset):
+        return lax.rem(region + offset + regions, regions)
+
+    steps = sorted(range(1, shards), key=lambda step: -min(step, shards - step))
+    peers = [lax.rem(shard + step, shards) for step in steps]
+    offsets = far_first(regions)
+    barrier = pltpu.get_barrier_semaphore()
+
+    def others(body):
+        for offset in offsets:
+            body(shifted(offset))
+
+    for peer in peers:
+        pl.semaphore_signal(barrier, inc=1, device_id=(region, peer), device_id_type=MESH)
+    others(lambda r: pl.semaphore_signal(barrier, inc=1, device_id=(r, shard), device_id_type=MESH))
 
     loads = [
         pltpu.make_async_copy(source, target, in_sem.at[i])
@@ -93,28 +124,14 @@
                 (weights_hbm, weights),
                 (inv_hbm.at[0], inv),
                 (interp_hbm.at[0], interp),
+                (cells_hbm, cells),
+                (points_hbm, points),
+                (neighbours_hbm, neighbours),
             ]
         )
     ]
-    for load in loads:
-        load.start()
-
-    def shifted(offset):
-        return lax.rem(region + offset + regions, regions)
-
-    peers = [lax.rem(shard + step, shards) for step in range(1, shards)]
-    barrier = pltpu.get_barrier_semaphore()
-
-    def others(body):
-        def one(offset, carry):
-            body(shifted(offset))
-            return carry
-
-        lax.fori_loop(1, regions, one, 0)
-
-    others(lambda r: pl.semaphore_signal(barrier, inc=1, device_id=(r, shard), device_id_type=MESH))
-    for peer in peers:
-        pl.semaphore_signal(barrier, inc=1, device_id=(region, peer), device_id_type=MESH)
+    for i in (5, 6, 0, 7, 1, 2):
+        loads[i].start()
 
     def remote(source, target, send, arrive, device):
         return pltpu.make_async_remote_copy(
@@ -154,12 +171,12 @@
         for turn in range(ITERS)
     ]
 
-    total = points[region]
-    stride = lax.rem(neighbours[2, 0] + regions, regions)
-    backward = jnp.where(region < regions // 2, regions - stride, stride)
+    def backward():
+        stride = lax.rem(neighbours[2, 0] + regions, regions)
+        return jnp.where(region < regions // 2, regions - stride, stride)
 
     def alive(n):
-        return jnp.where((shard * blocks + n) * BLK < total, f32(1.0), f32(0.0))
+        return jnp.where((shard * blocks + n) * BLK < points[region], f32(1.0), f32(0.0))
 
     def rows_of(n):
         return pl.ds(pl.multiple_of(n * BLK, BLK), BLK)
@@ -180,11 +197,13 @@
             copy.start()
 
     def send_part(turn, total_part):
-        part[turn] = total_part
+        for i in range(MOMENTS):
+            part[turn, i] = total_part[i : i + 1, :]
         for copy in part_copies[turn]:
             copy.start()
 
     with jax.named_scope("onehot"):
+        loads[5].wait()
         onehot_f[...] = jnp.zeros_like(onehot_f)
         lane = lax.broadcasted_iota(jnp.int32, (1, cell_count), 1)
         for k in range(NBR):
@@ -199,7 +218,10 @@
             halved[i * width : (i + 1) * width, :] = half
 
     with jax.named_scope("wait_dist"):
+        loads[6].wait()
         loads[0].wait()
+        loads[3].start()
+        loads[4].start()
 
     def first_edges(n, carry):
         high, low = halves(dist[rows_of(n), :] * alive(n))
@@ -217,6 +239,8 @@
     with jax.named_scope("basis"):
         loads[1].wait()
         loads[2].wait()
+        loads[7].wait()
+        total = points[region]
         x, y, z = vel[0], vel[1], vel[2]
         place = shard * local + lax.broadcasted_iota(jnp.int32, (1, local), 1)
         scale = f32(VMAX) / jnp.full((1, local), total.astype(f32))
@@ -262,8 +286,10 @@
     def forward(turn):
         all_tiles(turn, 0).wait_recv()
 
+        back = backward()
+
         def take(r, carry):
-            moved[turn, r] = hold[turn][lax.rem(r + backward, regions)]
+            moved[turn, r] = hold[turn][lax.rem(r + back, regions)]
             return carry
 
         lax.fori_loop(0, regions, take, 0, unroll=8)
@@ -299,11 +325,11 @@
     with jax.named_scope("prepare_inv"):
         loads[3].wait()
         each(prepare_inv)
-    with jax.named_scope("forward0"):
-        forward(0)
     with jax.named_scope("prepare_mat"):
         loads[4].wait()
         each(prepare_mat)
+    with jax.named_scope("forward0"):
+        forward(0)
 
     def collect(turn):
         for copy in part_copies[turn]:
@@ -311,7 +337,7 @@
         moments = part[turn]
         for j in range(shards - 1):
             moments = moments + gathered[turn, j]
-        rows = cell_rows([moments[i : i + 1, :] for i in range(13)])
+        rows = cell_rows([moments[i] for i in range(MOMENTS)])
         for i, row in enumerate(rows):
             coef[i : i + 1, :] = row
 
@@ -340,27 +366,34 @@
             pieces[n, k, 0:EDGE, BLK : 2 * BLK] = high[:, lanes]
             pieces[n, k, EDGE : 2 * EDGE, 0:BLK] = low[:, lanes]
 
-    def arrive(turn):
+    def interpolate(interfaces, done):
+        def one(n, carry):
+            for k in interfaces:
+                both = across(pieces[n, k], mats[n, k])
+                high, low = halves(both[:EDGE] + both[EDGE:])
+                flow_t[n, EDGE * k : EDGE * (k + 1)] = high
+                flow_t[n, width + EDGE * k : width + EDGE * (k + 1)] = low
+                flow_t[n, 2 * width + EDGE * k : 2 * width + EDGE * (k + 1)] = high
+            if done:
+                flow[n] = jnp.transpose(flow_t[n])
+            return carry
+
+        each(one)
+
+    def arrive_direct(turn):
         for j, k in enumerate((0, 1, 4)):
             direct_copies[turn][j].wait_recv()
             place_in(k, recv[turn, j])
+        interpolate((0, 1, 4), False)
+
+    def arrive(turn):
         all_tiles(turn, 1).wait_recv()
         for k, first in ((3, 0), (2, 2 * blocks)):
             rows = [[reached[turn, first + g * blocks + n] for n in range(blocks)] for g in range(2)]
             place_in(k, jnp.concatenate([jnp.concatenate(r, axis=1) for r in rows], axis=0))
 
-    def interpolate(n, carry):
-        flows = []
-        for k in range(NBR):
-            both = across(pieces[n, k], mats[n, k])
-            flows.append(both[:EDGE] + both[EDGE:])
-        high, low = halves(jnp.concatenate(flows, axis=0))
-        flow_t[n, 0:width] = high
-        flow_t[n, width : 2 * width] = low
-        flow_t[n, 2 * width : 3 * width] = high
-        flow[n] = jnp.transpose(flow_t[n])
-        return carry
-
+    with jax.named_scope("direct0"):
+        arrive_direct(0)
     with jax.named_scope("collect0"):
         collect(0)
     with jax.named_scope("relax0"):
@@ -392,7 +425,7 @@
     with jax.named_scope("arrive0"):
         arrive(0)
     with jax.named_scope("interpolate0"):
-        each(interpolate)
+        interpolate((2, 3), True)
 
     def landed_edges(n, carry):
         post_edges(1, n, (kept[n] + plain(edge_edge[n], flow_t[n])) * alive(n))
@@ -411,6 +444,8 @@
         send_part(1, each(landed_moments, main_part))
     with jax.named_scope("forward1"):
         forward(1)
+    with jax.named_scope("direct1"):
+        arrive_direct(1)
     with jax.named_scope("collect1"):
         collect(1)
     with jax.named_scope("relax1"):
@@ -418,13 +453,19 @@
 
     def main_result(n, carry):
         high, low = halves(rhs[rows_of(n), :])
-        value = across(jnp.concatenate([high, high], axis=1), both_inv[n])
-        result[rows_of(n), :] = value + across(low, both_inv[n, :, 0:cell_count])
+        wide = jnp.concatenate(
+            [
+                jnp.concatenate([high, high], axis=1),
+                jnp.concatenate([low, jnp.zeros_like(low)], axis=1),
+            ],
+            axis=0,
+        )
+        turned = across(both_inv[n], wide)
+        out[0, rows_of(n), :] = jnp.transpose(turned[:, :BLK] + turned[:, BLK:])
         return carry
 
     def last(n, carry):
-        result[rows_of(n), :] = (result[rows_of(n), :] + plain(flow[n], inv_edge[n])) * alive(n)
-        pltpu.make_async_copy(result.at[rows_of(n)], out_hbm.at[0, rows_of(n)], out_sem.at[n]).start()
+        out[0, rows_of(n), :] = (out[0, rows_of(n), :] + plain(flow[n], inv_edge[n])) * alive(n)
         return carry
 
     with jax.named_scope("main_result"):
@@ -432,13 +473,10 @@
     with jax.named_scope("arrive1"):
         arrive(1)
     with jax.named_scope("interpolate1"):
-        each(interpolate)
+        interpolate((2, 3), True)
     with jax.named_scope("last"):
         each(last)
     with jax.named_scope("finish"):
-        for n in range(blocks):
-            rows = pl.ds(n * BLK, BLK)
-            pltpu.make_async_copy(result.at[rows], out_hbm.at[0, rows], out_sem.at[n]).wait()
         for turn in range(ITERS):
             for copy in part_copies[turn] + direct_copies[turn]:
                 copy.wait_send()
@@ -452,15 +490,17 @@
     blocks = local // BLK
     width = NBR * EDGE
     anywhere = pl.BlockSpec(memory_space=pl.ANY)
-    scalars = pl.BlockSpec(memory_space=pltpu.SMEM)
     vmem = pltpu.VMEM
     signals = pltpu.SemaphoreType.DMA
     return pl.pallas_call(
         functools.partial(kernel, regions, shards, unroll),
         out_shape=jax.ShapeDtypeStruct((1, local, cell_count), f32),
-        in_specs=[anywhere, anywhere, anywhere, scalars, scalars, scalars, anywhere, anywhere],
-        out_specs=anywhere,
+        in_specs=[anywhere] * 8,
+        out_specs=pl.BlockSpec(memory_space=pltpu.VMEM),
         scratch_shapes=[
+            pltpu.SMEM(points.shape, jnp.int32),
+            pltpu.SMEM(neighbours.shape, jnp.int32),
+            pltpu.SMEM(cells.shape, jnp.int32),
             vmem((local, cell_count), f32),
             vmem((3, 1, local), f32),
             vmem((1, local), f32),
@@ -488,13 +528,11 @@
             vmem((regions, TILE, BLK), f32),
             vmem((ITERS, regions, TILE, BLK), f32),
             vmem((ITERS, regions, TILE, BLK), f32),
-            vmem((ITERS, BASIS, cell_count), f32),
-            vmem((ITERS, shards - 1, BASIS, cell_count), f32),
+            vmem((ITERS, MOMENTS, 1, cell_count), f32),
+            vmem((ITERS, shards - 1, MOMENTS, 1, cell_count), f32),
             vmem((8, cell_count), f32),
             vmem((local, cell_count), f32),
-            vmem((local, cell_count), f32),
-            signals((5,)),
-            signals((blocks,)),
+            signals((8,)),
             signals((ITERS, 3)),
             signals((ITERS, 3)),
             signals((ITERS, 2)),

time: 42.3 us -> 37.8 us (0.89)
  Pallas kernels: 39.5 us -> 35 us
    pallas_call x1, Pallas kernels: 39.5 us -> 35 us  [update(): pl.pallas_call(functools.partial(kernel, regions, shards, unroll), out_sh...]
where the time goes in v1:
time: 37.8 us; the launch traced here: 37.7 us
  Pallas kernels  35 us (93%)
  local copies, waits for them, and re-layouts  2.65 us (7%)
    pallas_call x1, Pallas kernels, update(): pl.pallas_call(functools.partial(kernel, regions, shards, unroll), out_sh...  35 us
    unnamed x1, local copies, waits for them, and re-layouts  2.65 us

profile of v1, /device:TPU:1, one launch (start us, length us, event | category | flops | bytes accessed | tf_op | source)
XLA Modules:
  0.0 37.7 jit_solution(1799403800707685379)
XLA Ops:
  0.0 35.0 %shard_map.82 = f32[1,1024,384]{2,1,0:T(8,128)} custom-call(f32[1,1024,384]{2,1,0:T(8,128)} %dist_hbm.1, f32[3,1,1024]{2,1,0:T(1,128)} %bitcast.3, f32[1,1024]{1,0:T(1,128)} %weights_hbm.1, s32[32]{0:T(128)} %points_hbm.1, s32[5,32]{1,0:T(8,128)} %bitcast.4, s32[5,1,16]{2,1,0:T(1,128)} %bitcast.5, f32[1,5,1024,128]{3,2,1,0:T(8,128)} %interp_hbm.1, ...), custom_call_target="tpu_custom_call" | custom-call | tf_op jit(solution)/shard_map/pallas_call | solution.py:495
  35.0 2.7 %copy.10 = f32[1,1024,384]{2,1,0:T(8,128)} copy(f32[1,1024,384]{2,1,0:T(8,128)} %shard_map.82) | data formatting | bytes 3145728

commit v2 on v1

--- a/solution.py
+++ b/solution.py
@@ -88,10 +88,10 @@
 
 def kernel(
     regions, shards, unroll,
-    dist_hbm, vel_hbm, weights_hbm, points_hbm, neighbours_hbm, cells_hbm, interp_hbm, inv_hbm, out,
+    dist_hbm, vel_hbm, weights_hbm, points_hbm, neighbours_hbm, cells_hbm, interp_hbm, inv_hbm, out_hbm,
     points, neighbours, cells, dist, vel, weights, interp, inv, both_inv, both_edge, edge_edge, inv_edge, mats,
-    basis_f, basis, columns, onehot_f, onehot, halved, pieces, flow_t, flow, kept, sent, recv, tiles, hold_a, hold_b, moved, reached, part, gathered, coef, rhs,
-    in_sem, edge_send, edge_recv, hop_send, hop_recv, part_send, part_recv,
+    basis_f, basis, columns, onehot_f, onehot, halved, spread, pieces, flow_t, flow, kept, sent, recv, tiles, hold_a, hold_b, moved, reached, part, gathered, coef, rhs, held, falls, out,
+    in_sem, out_sem, edge_send, edge_recv, hop_send, hop_recv, part_send, part_recv,
 ):
     region = lax.axis_index("region")
     shard = lax.axis_index("vel")
@@ -214,6 +214,9 @@
         onehot[...] = picks.astype(bf16)
         half = (inflow_step * picks[0:width]).astype(bf16)
         halved[3 * width :, :] = jnp.zeros((WIDE - 3 * width, cell_count), bf16)
+        spread[2 * width :, :] = jnp.zeros((WIDE - 2 * width, cell_count), bf16)
+        for i in range(2):
+            spread[i * width : (i + 1) * width, :] = half
         for i in range(3):
             halved[i * width : (i + 1) * width, :] = half
 
@@ -226,7 +229,8 @@
     def first_edges(n, carry):
         high, low = halves(dist[rows_of(n), :] * alive(n))
         pick = onehot[0:width]
-        post_edges(0, n, across(pick, high) + across(pick, low))
+        twice = jnp.concatenate([pick, pick], axis=1)
+        post_edges(0, n, across(twice, jnp.concatenate([high, low], axis=1)))
         return carry
 
     with jax.named_scope("first_edges"):
@@ -305,14 +309,25 @@
         both_edge[n, 0:width, cell_count : 2 * cell_count] = edges[:, 0:cell_count]
         both_edge[n, width : 2 * width, 0:cell_count] = edges[:, cell_count : 2 * cell_count]
         both_edge[n, width : 2 * width, cell_count : 2 * cell_count] = jnp.zeros((width, cell_count), bf16)
-        back_h = across(halved[0:width], high).astype(bf16)
+        return carry
+
+    def prepare_edge_edge(group, carry):
+        rows = both_edge[pl.ds(2 * group, 2), :, 0:cell_count].reshape(4 * width, cell_count)
+        value = across(rows, halved[...])
+        lane = lax.broadcasted_iota(jnp.int32, (width, WIDE), 1)
+        for i in range(2):
+            near = value[2 * i * width : (2 * i + 1) * width]
+            fine = value[(2 * i + 1) * width : (2 * i + 2) * width]
+            edge_edge[2 * group + i] = jnp.where(lane < 2 * width, near, fine).astype(bf16)
+        return carry
+
+    def prepare_inv_edge(n, carry):
+        back_h = across(halved[0:width], both_inv[n, :, 0:cell_count]).astype(bf16)
         inv_edge[n, 0:width] = back_h
         inv_edge[n, width : 2 * width] = back_h
-        inv_edge[n, 2 * width : WIDE] = across(halved[2 * width : WIDE], low).astype(bf16)
-        near = across(edges[:, 0:cell_count], halved[...])
-        fine = across(edges[:, cell_count : 2 * cell_count], halved[...])
-        lane = lax.broadcasted_iota(jnp.int32, (width, WIDE), 1)
-        edge_edge[n] = jnp.where(lane < 2 * width, near, fine).astype(bf16)
+        inv_edge[n, 2 * width : WIDE] = across(
+            halved[2 * width : WIDE], both_inv[n, :, cell_count : 2 * cell_count]
+        ).astype(bf16)
         return carry
 
     def prepare_mat(n, carry):
@@ -325,11 +340,12 @@
     with jax.named_scope("prepare_inv"):
         loads[3].wait()
         each(prepare_inv)
+        lax.fori_loop(0, blocks // 2, prepare_edge_edge, 0, unroll=unroll)
+    with jax.named_scope("forward0"):
+        forward(0)
     with jax.named_scope("prepare_mat"):
         loads[4].wait()
         each(prepare_mat)
-    with jax.named_scope("forward0"):
-        forward(0)
 
     def collect(turn):
         for copy in part_copies[turn]:
@@ -405,23 +421,17 @@
         kept[n] = edges[:width] + edges[width:]
         return carry
 
-    def main_moments(n, acc):
+    def main_moments(n, carry):
         high, low = halves(rhs[rows_of(n), :])
-        held_h, held_l = halves(weighted(n, high, low))
-        held = jnp.concatenate(
-            [
-                jnp.concatenate([held_h, held_h], axis=1),
-                jnp.concatenate([held_l, jnp.zeros_like(held_l)], axis=1),
-            ],
-            axis=0,
-        )
-        both = across(held, both_inv[n])
-        return acc + both[:BASIS] + both[BASIS:]
+        held[n] = weighted(n, high, low)
+        return carry
 
     with jax.named_scope("main_edges"):
         each(main_edges)
     with jax.named_scope("main_moments"):
-        main_part = each(main_moments, jnp.zeros((BASIS, cell_count), f32))
+        each(main_moments)
+    with jax.named_scope("inv_edge0"):
+        lax.fori_loop(0, blocks // 2, prepare_inv_edge, 0, unroll=unroll)
     with jax.named_scope("arrive0"):
         arrive(0)
     with jax.named_scope("interpolate0"):
@@ -431,17 +441,41 @@
         post_edges(1, n, (kept[n] + plain(edge_edge[n], flow_t[n])) * alive(n))
         return carry
 
-    def landed_moments(n, acc):
+    def fall_moments(n, carry):
         both = plain(basis[n, :, 0:BLK], flow[n])
-        held_h, held_l = halves(both[:BASIS] + both[BASIS:])
-        both = plain(jnp.concatenate([held_h, held_l], axis=0), inv_edge[n])
-        return acc + both[:BASIS] + both[BASIS:]
+        fall_h, fall_l = halves(both[:BASIS] + both[BASIS:])
+        falls[n, 0:BASIS] = fall_h
+        falls[n, BASIS : 2 * BASIS] = fall_l
+        return carry
+
+    def landed_moments():
+        each(fall_moments)
+        spreads = plain(falls[...].reshape(2 * BASIS * blocks, WIDE), spread[...])
+        acc = jnp.zeros((BASIS, cell_count), f32)
+        for n in range(blocks):
+            start = 2 * BASIS * n
+            both = spreads[start : start + BASIS] + spreads[start + BASIS : start + 2 * BASIS]
+            held_h, held_l = halves(held[n] + both)
+            both = across(
+                jnp.concatenate(
+                    [
+                        jnp.concatenate([held_h, held_h], axis=1),
+                        jnp.concatenate([held_l, jnp.zeros_like(held_l)], axis=1),
+                    ],
+                    axis=0,
+                ),
+                both_inv[n],
+            )
+            acc = acc + both[:BASIS] + both[BASIS:]
+        return acc
 
     with jax.named_scope("landed_edges"):
         each(landed_edges)
         send_edges(1)
     with jax.named_scope("landed_moments"):
-        send_part(1, each(landed_moments, main_part))
+        send_part(1, landed_moments())
+    with jax.named_scope("inv_edge1"):
+        lax.fori_loop(blocks // 2, blocks, prepare_inv_edge, 0, unroll=unroll)
     with jax.named_scope("forward1"):
         forward(1)
     with jax.named_scope("direct1"):
@@ -461,11 +495,12 @@
             axis=0,
         )
         turned = across(both_inv[n], wide)
-        out[0, rows_of(n), :] = jnp.transpose(turned[:, :BLK] + turned[:, BLK:])
+        out[rows_of(n), :] = jnp.transpose(turned[:, :BLK] + turned[:, BLK:])
         return carry
 
     def last(n, carry):
-        out[0, rows_of(n), :] = (out[0, rows_of(n), :] + plain(flow[n], inv_edge[n])) * alive(n)
+        out[rows_of(n), :] = (out[rows_of(n), :] + plain(flow[n], inv_edge[n])) * alive(n)
+        pltpu.make_async_copy(out.at[rows_of(n)], out_hbm.at[0, rows_of(n)], out_sem.at[n]).start()
         return carry
 
     with jax.named_scope("main_result"):
@@ -477,11 +512,28 @@
     with jax.named_scope("last"):
         each(last)
     with jax.named_scope("finish"):
+        for n in range(blocks):
+            pltpu.make_async_copy(out.at[rows_of(n)], out_hbm.at[0, rows_of(n)], out_sem.at[n]).wait()
         for turn in range(ITERS):
             for copy in part_copies[turn] + direct_copies[turn]:
                 copy.wait_send()
             for step in range(2):
                 all_tiles(turn, step).wait_send()
+
+
+def hand_on(value_hbm, out_hbm, held, in_sems, out_sems):
+    parts = in_sems.shape[0]
+    rows = held.shape[0] // parts
+    ways = [pl.ds(i * rows, rows) for i in range(parts)]
+    takes = [pltpu.make_async_copy(value_hbm.at[0, way], held.at[way], in_sems.at[i]) for i, way in enumerate(ways)]
+    gives = [pltpu.make_async_copy(held.at[way], out_hbm.at[0, way], out_sems.at[i]) for i, way in enumerate(ways)]
+    for take in takes:
+        take.start()
+    for take, give in zip(takes, gives):
+        take.wait()
+        give.start()
+    for give in gives:
+        give.wait()
 
 
 def update(regions, shards, unroll, *arrays):
@@ -492,11 +544,11 @@
     anywhere = pl.BlockSpec(memory_space=pl.ANY)
     vmem = pltpu.VMEM
     signals = pltpu.SemaphoreType.DMA
-    return pl.pallas_call(
+    value = pl.pallas_call(
         functools.partial(kernel, regions, shards, unroll),
         out_shape=jax.ShapeDtypeStruct((1, local, cell_count), f32),
         in_specs=[anywhere] * 8,
-        out_specs=pl.BlockSpec(memory_space=pltpu.VMEM),
+        out_specs=anywhere,
         scratch_shapes=[
             pltpu.SMEM(points.shape, jnp.int32),
             pltpu.SMEM(neighbours.shape, jnp.int32),
@@ -517,6 +569,7 @@
             vmem((PAD, cell_count), f32),
             vmem((PAD, cell_count), bf16),
             vmem((WIDE, cell_count), bf16),
+            vmem((WIDE, cell_count), bf16),
             vmem((blocks, NBR, 2 * EDGE, 2 * BLK), bf16),
             vmem((blocks, WIDE, BLK), bf16),
             vmem((blocks, BLK, WIDE), bf16),
@@ -532,7 +585,11 @@
             vmem((ITERS, shards - 1, MOMENTS, 1, cell_count), f32),
             vmem((8, cell_count), f32),
             vmem((local, cell_count), f32),
+            vmem((blocks, BASIS, cell_count), f32),
+            vmem((blocks, 2 * BASIS, WIDE), bf16),
+            vmem((local, cell_count), f32),
             signals((8,)),
+            signals((blocks,)),
             signals((ITERS, 3)),
             signals((ITERS, 3)),
             signals((ITERS, 2)),
@@ -544,6 +601,14 @@
             collective_id=0, has_side_effects=True, vmem_limit_bytes=56 * 1024 * 1024
         ),
     )(distribution, velocity, weights, points, neighbours, cells, interpolation, inverse)
+    return pl.pallas_call(
+        hand_on,
+        out_shape=jax.ShapeDtypeStruct(value.shape, f32),
+        in_specs=[anywhere],
+        out_specs=anywhere,
+        scratch_shapes=[vmem((local, cell_count), f32), signals((8,)), signals((8,))],
+        compiler_params=pltpu.CompilerParams(vmem_limit_bytes=56 * 1024 * 1024),
+    )(value)
 
 
 def solution(mesh):

time: 37.8 us -> 36.3 us (0.960)
  local copies, waits for them, and re-layouts: 2.65 us -> 0 us
  Pallas kernels: 35 us -> 36.1 us
    unnamed x1 -> x0, local copies, waits for them, and re-layouts: 2.65 us -> none
    pallas_call x0 -> x1, Pallas kernels: none -> 2.29 us  [update(): pl.pallas_call(hand_on, out_shape=jax.ShapeDtypeStruct(value.shape, f32),...]
    pallas_call x1, Pallas kernels: 35 us -> 33.8 us  [update(): pl.pallas_call(functools.partial(kernel, regions, shards, unroll), out_sh...]
where the time goes in v2:
time: 36.3 us; the launch traced here: 36.1 us
  Pallas kernels  36.1 us (99%)
    pallas_call x1, Pallas kernels, update(): pl.pallas_call(functools.partial(kernel, regions, shards, unroll), out_sh...  33.8 us
    pallas_call x1, Pallas kernels, update(): pl.pallas_call(hand_on, out_shape=jax.ShapeDtypeStruct(value.shape, f32),...  2.29 us

profile of v2, /device:TPU:1, one launch (start us, length us, event | category | flops | bytes accessed | tf_op | source)
XLA Modules:
  0.0 36.1 jit_solution(6281839933459334412)
XLA Ops:
  0.0 33.8 %shard_map.82.value_hbm = f32[1,1024,384]{2,1,0:T(8,128)} custom-call(f32[1,1024,384]{2,1,0:T(8,128)} %dist_hbm.1, f32[3,1,1024]{2,1,0:T(1,128)} %bitcast.3, f32[1,1024]{1,0:T(1,128)} %weights_hbm.1, s32[32]{0:T(128)} %points_hbm.1, s32[5,32]{1,0:T(8,128)} %bitcast.4, s32[5,1,16]{2,1,0:T(1,128)} %bitcast.5, f32[1,5,1024,128]{3,2,1,0:T(8,128)} %interp_hbm.1, ...), custom_call_target="tpu_custom_call" | custom-call | tf_op jit(solution)/shard_map/pallas_call | solution.py:547
  33.9 2.3 %shard_map.83 = f32[1,1024,384]{2,1,0:T(8,128)} custom-call(f32[1,1024,384]{2,1,0:T(8,128)} %shard_map.82.value_hbm), custom_call_target="tpu_custom_call" | custom-call | tf_op jit(solution)/shard_map/pallas_call | solution.py:604

commit v3 on v2

--- a/solution.py
+++ b/solution.py
@@ -341,11 +341,11 @@
         loads[3].wait()
         each(prepare_inv)
         lax.fori_loop(0, blocks // 2, prepare_edge_edge, 0, unroll=unroll)
-    with jax.named_scope("forward0"):
-        forward(0)
     with jax.named_scope("prepare_mat"):
         loads[4].wait()
         each(prepare_mat)
+    with jax.named_scope("forward0"):
+        forward(0)
 
     def collect(turn):
         for copy in part_copies[turn]:
@@ -435,14 +435,14 @@
     with jax.named_scope("arrive0"):
         arrive(0)
     with jax.named_scope("interpolate0"):
-        interpolate((2, 3), True)
+        interpolate((2, 3), False)
 
     def landed_edges(n, carry):
         post_edges(1, n, (kept[n] + plain(edge_edge[n], flow_t[n])) * alive(n))
         return carry
 
     def fall_moments(n, carry):
-        both = plain(basis[n, :, 0:BLK], flow[n])
+        both = plain(basis[n, :, 0:BLK], jnp.transpose(flow_t[n]))
         fall_h, fall_l = halves(both[:BASIS] + both[BASIS:])
         falls[n, 0:BASIS] = fall_h
         falls[n, BASIS : 2 * BASIS] = fall_l

time: 36.3 us -> 36 us (level)
  no operation moved by 1% of the time
where the time goes in v3:
time: 36 us; the launch traced here: 35.9 us
  Pallas kernels  35.8 us (99%)
    pallas_call x1, Pallas kernels, update(): pl.pallas_call(functools.partial(kernel, regions, shards, unroll), out_sh...  33.6 us
    pallas_call x1, Pallas kernels, update(): pl.pallas_call(hand_on, out_shape=jax.ShapeDtypeStruct(value.shape, f32),...  2.29 us

profile of v3, /device:TPU:1, one launch (start us, length us, event | category | flops | bytes accessed | tf_op | source)
XLA Modules:
  0.0 35.9 jit_solution(7292005759765442119)
XLA Ops:
  0.0 33.6 %shard_map.82.value_hbm = f32[1,1024,384]{2,1,0:T(8,128)} custom-call(f32[1,1024,384]{2,1,0:T(8,128)} %dist_hbm.1, f32[3,1,1024]{2,1,0:T(1,128)} %bitcast.3, f32[1,1024]{1,0:T(1,128)} %weights_hbm.1, s32[32]{0:T(128)} %points_hbm.1, s32[5,32]{1,0:T(8,128)} %bitcast.4, s32[5,1,16]{2,1,0:T(1,128)} %bitcast.5, f32[1,5,1024,128]{3,2,1,0:T(8,128)} %interp_hbm.1, ...), custom_call_target="tpu_custom_call" | custom-call | tf_op jit(solution)/shard_map/pallas_call | solution.py:547
  33.6 2.3 %shard_map.83 = f32[1,1024,384]{2,1,0:T(8,128)} custom-call(f32[1,1024,384]{2,1,0:T(8,128)} %shard_map.82.value_hbm), custom_call_target="tpu_custom_call" | custom-call | tf_op jit(solution)/shard_map/pallas_call | solution.py:604
